TPU v7x, 32 devices: a whole 2x2x4 slice. The times are simulated.
32 devices in a mesh: groups: 1, blk: 16 (over z, y, x), heads: 2 (over core).
Axes of the slice: x: 2, y: 2, z: 4, core: 2. Of those that a mesh axis runs over, the one named last changes fastest.
Arguments:
- queries: bfloat16 [4096, 2048], P(('groups', 'blk', 'heads')), may hold values from -186 to 186
- keys: bfloat16 [4096, 1024], P(('groups', 'blk', 'heads')), may hold values from -6 to 6
- values: bfloat16 [4096, 1024], P(('groups', 'blk', 'heads')), may hold values from -6 to 6
- upstream: bfloat16 [4096, 2048], P(('groups', 'blk', 'heads')), may hold values from -6 to 6
- doc_ids: int32 [32], P('groups'), may hold values from 0 to 3, never falling along the last dimension, each value on 1 to 16 neighbouring positions
- band: int32 [32], P('groups'), may hold values from 0 to 8, as said below
Outputs:
- query_grad: bfloat16 [4096, 2048], P(('groups', 'blk', 'heads'))
- key_gradient: bfloat16 [4096, 1024], P(('groups', 'blk', 'heads'))
- value_gradient: bfloat16 [4096, 1024], P(('groups', 'blk', 'heads'))
Inputs may be any that keep to these rules, and one draw needn't show every extreme that they name: `band`: earlier blocks a query block may see; some block sees 8 and some sees 0.
All inputs are finite; a program needn't handle non-finite values.
Results may differ from a plain program's by a relative error of at most 0.0083.
Values may be sent and summed in bfloat16 or wider, within the bound.
No kernel may reach another device: no remote copies, remote signals or barrier semaphores. Data moves between devices by JAX's collectives and lax.ppermute only.
A program may use at most 64 MiB of HBM per device.

v0:
```python
import jax
import jax.numpy as jnp
from jax import lax
from jax.sharding import PartitionSpec as P

HEAD_SIZE = 128
SCALAR = 168
WINDOW_TOKENS = 1024
MASK_BLOCK = 128


def from_behind(value, axis, steps):
    count = lax.axis_size(axis)
    leading, last = (max(0, -steps), min(count, count - steps))
    return lax.ppermute(value, axis, [(source, source + steps) for source in range(leading, last)])


def attend_group(operands, allowed):
    query_part, key_part, value_part, grad_part = operands
    scale = SCALAR ** (-0.5)
    scores = (
        jnp.einsum("hqd,kd->hqk", query_part, key_part, preferred_element_type=jnp.float32) * scale
    )
    scores = jnp.where(allowed, scores, -jnp.inf)
    top = jnp.max(scores, axis=-1, keepdims=True)
    expo = jnp.exp(scores - top)
    probs = expo / jnp.sum(expo, axis=-1, keepdims=True)
    probs_b = probs.astype(jnp.bfloat16)
    output = jnp.einsum("hqk,kd->hqd", probs_b, value_part, preferred_element_type=jnp.float32)
    delta = jnp.sum(grad_part.astype(jnp.float32) * output, axis=-1)
    dprob = jnp.einsum("hqd,kd->hqk", grad_part, value_part, preferred_element_type=jnp.float32)
    dscore = (probs * (dprob - delta[..., None])).astype(jnp.bfloat16)
    query_grad = (
        jnp.einsum("hqk,kd->hqd", dscore, key_part, preferred_element_type=jnp.float32) * scale
    )
    key_gradient = (
        jnp.einsum("hqk,hqd->kd", dscore, query_part, preferred_element_type=jnp.float32) * scale
    )
    value_gradient = jnp.einsum(
        "hqk,hqd->kd", probs_b, grad_part, preferred_element_type=jnp.float32
    )
    return (query_grad, key_gradient, value_gradient)


def visible_mask(doc_ids, band, span):
    window_blocks = WINDOW_TOKENS // MASK_BLOCK
    query_blocks = span // MASK_BLOCK
    key_blocks = (WINDOW_TOKENS + span) // MASK_BLOCK
    first = lax.axis_index("blk") * query_blocks
    doc_pad = jnp.concatenate([jnp.full((window_blocks,), -1, jnp.int32), doc_ids])
    query_docs = lax.dynamic_slice_in_dim(doc_ids, first, query_blocks, 0)
    query_band = lax.dynamic_slice_in_dim(band, first, query_blocks, 0)
    key_docs = lax.dynamic_slice_in_dim(doc_pad, first, key_blocks, 0)
    query_pos = jnp.arange(query_blocks, dtype=jnp.int32)
    key_pos = jnp.arange(key_blocks, dtype=jnp.int32)
    block_ok = (query_docs[:, None] == key_docs[None, :]) & (
        query_pos[:, None] + window_blocks - key_pos[None, :] <= query_band[:, None]
    )
    expanded = jnp.broadcast_to(
        block_ok[:, None, :, None], (query_blocks, MASK_BLOCK, key_blocks, MASK_BLOCK)
    ).reshape(span, WINDOW_TOKENS + span)
    causal = (
        jnp.arange(WINDOW_TOKENS + span, dtype=jnp.int32)[None, :]
        <= jnp.arange(span, dtype=jnp.int32)[:, None] + WINDOW_TOKENS
    )
    return expanded & causal


def per_device(queries, keys, values, upstream, doc_ids, band):
    query_row_slice = lax.all_to_all(queries, "heads", split_axis=1, concat_axis=0, tiled=True)
    key_row_slice, value_row_slice = (
        lax.all_to_all(keys, "heads", split_axis=1, concat_axis=0, tiled=True),
        lax.all_to_all(values, "heads", split_axis=1, concat_axis=0, tiled=True),
    )
    gradient_rows = lax.all_to_all(upstream, "heads", split_axis=1, concat_axis=0, tiled=True)
    span = query_row_slice.shape[0]
    width = key_row_slice.shape[1]
    kv_heads = width // HEAD_SIZE
    q_heads = query_row_slice.shape[1] // HEAD_SIZE
    group_ratio = q_heads // kv_heads
    reach = max(1, WINDOW_TOKENS // span)
    span_extent = WINDOW_TOKENS + span
    paired = jnp.concatenate([key_row_slice, value_row_slice], axis=1)
    earlier = [from_behind(paired, "blk", offset) for offset in range(reach, 0, -1)]
    window_rows = jnp.concatenate(earlier + [paired], axis=0)
    allowed = visible_mask(doc_ids, band, span)
    query_groups = query_row_slice.reshape(span, kv_heads, group_ratio, HEAD_SIZE).transpose(
        1, 2, 0, 3
    )
    grad_groups = gradient_rows.reshape(span, kv_heads, group_ratio, HEAD_SIZE).transpose(
        1, 2, 0, 3
    )
    key_groups = window_rows[:, :width].reshape(span_extent, kv_heads, HEAD_SIZE).transpose(1, 0, 2)
    value_groups = (
        window_rows[:, width:].reshape(span_extent, kv_heads, HEAD_SIZE).transpose(1, 0, 2)
    )
    query_terms, key_terms, value_terms = lax.map(
        lambda operands: attend_group(operands, allowed),
        (query_groups, key_groups, value_groups, grad_groups),
    )
    query_grad = (
        query_terms.transpose(2, 0, 1, 3).reshape(span, q_heads * HEAD_SIZE).astype(jnp.bfloat16)
    )
    key_flat = key_terms.transpose(1, 0, 2).reshape(span_extent, width)
    value_flat = value_terms.transpose(1, 0, 2).reshape(span_extent, width)
    combined = jnp.concatenate([key_flat, value_flat], axis=1)
    own = combined[WINDOW_TOKENS:]
    spill = combined[:WINDOW_TOKENS]
    total = own
    for offset in range(1, reach + 1):
        total = total + from_behind(
            spill[(reach - offset) * span : (reach - offset + 1) * span], "blk", -offset
        )
    key_gradient = total[:, :width].astype(jnp.bfloat16)
    value_gradient = total[:, width:].astype(jnp.bfloat16)
    query_out, key_out, value_out = (
        lax.all_to_all(query_grad, "heads", split_axis=0, concat_axis=1, tiled=True),
        lax.all_to_all(key_gradient, "heads", split_axis=0, concat_axis=1, tiled=True),
        lax.all_to_all(value_gradient, "heads", split_axis=0, concat_axis=1, tiled=True),
    )
    return (query_out, key_out, value_out)


def solution(mesh):
    in_specs = (
        P(("groups", "blk", "heads"), None),
        P(("groups", "blk", "heads"), None),
        P(("groups", "blk", "heads"), None),
        P(("groups", "blk", "heads"), None),
        P("groups"),
        P("groups"),
    )
    out_specs = (
        P(("groups", "blk", "heads"), None),
        P(("groups", "blk", "heads"), None),
        P(("groups", "blk", "heads"), None),
    )
    return jax.shard_map(
        per_device, mesh=mesh, in_specs=in_specs, out_specs=out_specs, check_vma=False
    )
```

profile of v0, /device:TPU:19, one launch (start us, length us, event | category | flops | bytes accessed | tf_op | source)
XLA Modules:
  0.0 265.9 jit_solution(4119912170533219803)
XLA Ops:
  0.6 1.8 copy.35
  2.5 4.1 %all-to-all-start.1 = ((bf16[128,2,512]{0,2,1:T(8,128)(2,1)}), bf16[128,2,512]{0,2,1:T(8,128)(2,1)S(1)}, u32[]{:S(2)}, u32[]{:S(2)}) async-start(bf16[128,2,512]{0,2,1:T(8,128)(2,1)} %bitcast.2), calls=%async_computation.1 | async-start | bytes 524288 | tf_op jit(solution)/shard_map/all_to_all | solution.py:72
  6.6 1.8 copy.37
  8.5 3.5 %all-to-all-start.2 = ((bf16[128,2,512]{0,2,1:T(8,128)(2,1)}), bf16[128,2,512]{0,2,1:T(8,128)(2,1)S(1)}, u32[]{:S(2)}, u32[]{:S(2)}) async-start(bf16[128,2,512]{0,2,1:T(8,128)(2,1)} %bitcast.5), calls=%async_computation.2 | async-start | bytes 524288 | tf_op jit(solution)/shard_map/all_to_all | solution.py:73
  12.1 1.0 all-to-all-done.2
  13.3 0.9 pad_maximum_fusion.1
  14.2 3.1 %collective-permute-start.3 = (bf16[256,1024]{1,0:T(8,128)(2,1)}, bf16[256,1024]{1,0:T(8,128)(2,1)S(1)}, u32[]{:S(2)}, u32[]{:S(2)}) collective-permute-start(bf16[256,1024]{1,0:T(8,128)(2,1)} %pad_maximum_fusion.1), channel_id=1, source_target_pairs={{0,2},{2,4},{4,6},{6,8},{8,10},{10,12},{12,14},{14,16},{16,18},{18... | collective-permute-start | bytes 1572872 | tf_op jit(solution)/shard_map/ppermute | solution.py:15
  17.3 3.1 %collective-permute-start.2 = (bf16[256,1024]{1,0:T(8,128)(2,1)}, bf16[256,1024]{1,0:T(8,128)(2,1)}, u32[]{:S(2)}, u32[]{:S(2)}) collective-permute-start(bf16[256,1024]{1,0:T(8,128)(2,1)} %pad_maximum_fusion.1), channel_id=1, source_target_pairs={{0,4},{2,6},{4,8},{6,10},{8,12},{10,14},{12,16},{14,18},{16,20},{1... | collective-permute-start | bytes 1572872 | tf_op jit(solution)/shard_map/ppermute | solution.py:15
  20.5 3.2 %collective-permute-start.1 = (bf16[256,1024]{1,0:T(8,128)(2,1)}, bf16[256,1024]{1,0:T(8,128)(2,1)}, u32[]{:S(2)}, u32[]{:S(2)}) collective-permute-start(bf16[256,1024]{1,0:T(8,128)(2,1)} %pad_maximum_fusion.1), channel_id=1, source_target_pairs={{0,6},{2,8},{4,10},{6,12},{8,14},{10,16},{12,18},{14,20},{16,22},{... | collective-permute-start | bytes 1572872 | tf_op jit(solution)/shard_map/ppermute | solution.py:15
  23.6 1.9 collective-permute-start
  25.6 0.8 copy.99
  26.4 4.7 %all-to-all-start = ((bf16[128,2,1024]{2,0,1:T(8,128)(2,1)}), bf16[128,2,1024]{2,0,1:T(8,128)(2,1)S(1)}, u32[]{:S(2)}, u32[]{:S(2)}) async-start(bf16[128,2,1024]{2,0,1:T(8,128)(2,1)} %bitcast.120), calls=%async_computation | async-start | bytes 1048576 | tf_op jit(solution)/shard_map/all_to_all | solution.py:70
  31.4 0.9 copy.98
  32.5 3.8 %all-to-all-start.3 = ((bf16[128,2,1024]{2,0,1:T(8,128)(2,1)}), bf16[128,2,1024]{2,0,1:T(8,128)(2,1)S(1)}, u32[]{:S(2)}, u32[]{:S(2)}) async-start(bf16[128,2,1024]{2,0,1:T(8,128)(2,1)} %bitcast.119), calls=%async_computation.3 | async-start | bytes 1048576 | tf_op jit(solution)/shard_map/all_to_all | solution.py:75
  36.7 1.0 all-to-all-done.3
  37.7 1.2 reshape.131
  38.9 7.6 %collective-permute-done = bf16[256,1024]{1,0:T(8,128)(2,1)} collective-permute-done((bf16[256,1024]{1,0:T(8,128)(2,1)}, bf16[256,1024]{1,0:T(8,128)(2,1)}, u32[]{:S(2)}, u32[]{:S(2)}) %collective-permute-start) | collective-permute-done | bytes 524320 | tf_op jit(solution)/shard_map/ppermute | solution.py:15
  46.5 1.1 constant_dynamic-update-slice_fusion.5
  47.6 10.1 %collective-permute-done.1 = bf16[256,1024]{1,0:T(8,128)(2,1)} collective-permute-done((bf16[256,1024]{1,0:T(8,128)(2,1)}, bf16[256,1024]{1,0:T(8,128)(2,1)}, u32[]{:S(2)}, u32[]{:S(2)}) %collective-permute-start.1) | collective-permute-done | bytes 524320 | tf_op jit(solution)/shard_map/ppermute | solution.py:15
  57.6 1.1 constant_dynamic-update-slice_fusion.4
  58.7 1.1 constant_dynamic-update-slice_fusion.3
  60.1 1.5 copy.41
  62.2 60.1 %while.15 = (s32[]{:T(128)}, bf16[4,2,256,128]{3,2,1,0:T(8,128)(2,1)}, f32[4,1280,128]{1,2,0:T(8,128)}, f32[4,1280,128]{1,2,0:T(8,128)}, bf16[4,2,256,128]{3,1,0...) while((s32[]{:T(128)}, ...), condition=%wide.region_4.5_spmd.clone, body=%wide.region_0.4_spmd.clone.sunk | while | flops 1355059456 | bytes 27148552 | solution.py:97
  62.2 1.2 constant_dynamic-slice_fusion.3
  64.1 2.5 fusion.91
  66.5 2.7 %fusion.92 = f32[2,256]{1,0:T(2,128)S(1)} fusion(bf16[4,1280,128]{1,2,0:T(8,128)(2,1)} %get-tuple-element.232, s32[]{:T(128)S(6)} %copy.129, bf16[1,2,256,128]{3,1,0,2:T(2,128)(2,1)S(1)} %get-tuple-element.199, f32[2,256]{1,0:T(2,128)S(1)} %get-tuple-element.201, pred[256,1280]{1,0:T(8,128)(4,1)S(1)} %fusion.90, ...), kind=kOutput, calls=%fused_computation.21.clone.1 | convolution fusion | flops 339019008 | bytes 1250304 | tf_op jit(solution)/shard_map/while/body/eval_jaxpr/hqk,kd->hqd/dot_general | solution.py:29
  69.3 2.4 fusion.93
  73.9 0.9 constant_dynamic-update-slice_fusion.7
  74.8 2.5 fusion.96
  77.3 1.2 constant_dynamic-slice_fusion.3
  79.1 2.5 fusion.91
  81.5 2.7 %fusion.92 = f32[2,256]{1,0:T(2,128)S(1)} fusion(bf16[4,1280,128]{1,2,0:T(8,128)(2,1)} %get-tuple-element.232, s32[]{:T(128)S(6)} %copy.129, bf16[1,2,256,128]{3,1,0,2:T(2,128)(2,1)S(1)} %get-tuple-element.199, f32[2,256]{1,0:T(2,128)S(1)} %get-tuple-element.201, pred[256,1280]{1,0:T(8,128)(4,1)S(1)} %fusion.90, ...), kind=kOutput, calls=%fused_computation.21.clone.1 | convolution fusion | flops 339019008 | bytes 1250304 | tf_op jit(solution)/shard_map/while/body/eval_jaxpr/hqk,kd->hqd/dot_general | solution.py:29
  84.3 2.4 fusion.93
  88.9 0.9 constant_dynamic-update-slice_fusion.7
  89.8 2.5 fusion.96
  92.3 1.2 constant_dynamic-slice_fusion.3
  94.1 2.5 fusion.91
  96.5 2.7 %fusion.92 = f32[2,256]{1,0:T(2,128)S(1)} fusion(bf16[4,1280,128]{1,2,0:T(8,128)(2,1)} %get-tuple-element.232, s32[]{:T(128)S(6)} %copy.129, bf16[1,2,256,128]{3,1,0,2:T(2,128)(2,1)S(1)} %get-tuple-element.199, f32[2,256]{1,0:T(2,128)S(1)} %get-tuple-element.201, pred[256,1280]{1,0:T(8,128)(4,1)S(1)} %fusion.90, ...), kind=kOutput, calls=%fused_computation.21.clone.1 | convolution fusion | flops 339019008 | bytes 1250304 | tf_op jit(solution)/shard_map/while/body/eval_jaxpr/hqk,kd->hqd/dot_general | solution.py:29
  99.3 2.4 fusion.93
  103.9 0.9 constant_dynamic-update-slice_fusion.7
  104.8 2.5 fusion.96
  107.3 1.2 constant_dynamic-slice_fusion.3
  109.1 2.5 fusion.91
  111.5 2.7 %fusion.92 = f32[2,256]{1,0:T(2,128)S(1)} fusion(bf16[4,1280,128]{1,2,0:T(8,128)(2,1)} %get-tuple-element.232, s32[]{:T(128)S(6)} %copy.129, bf16[1,2,256,128]{3,1,0,2:T(2,128)(2,1)S(1)} %get-tuple-element.199, f32[2,256]{1,0:T(2,128)S(1)} %get-tuple-element.201, pred[256,1280]{1,0:T(8,128)(4,1)S(1)} %fusion.90, ...), kind=kOutput, calls=%fused_computation.21.clone.1 | convolution fusion | flops 339019008 | bytes 1250304 | tf_op jit(solution)/shard_map/while/body/eval_jaxpr/hqk,kd->hqd/dot_general | solution.py:29
  114.3 2.4 fusion.93
  118.9 0.9 constant_dynamic-update-slice_fusion.7
  119.8 2.5 fusion.96
  122.3 4.4 %fusion.54 = (f32[256,1024]{0,1:T(8,128)}, f32[256,1024]{0,1:T(8,128)}, f32[256,1024]{0,1:T(8,128)}, f32[256,1024]{0,1:T(8,128)}) fusion(f32[1280,512]{0,1:T(8,128)} %bitcast.166, f32[1280,512]{0,1:T(8,128)} %bitcast.164), kind=kLoop, calls=%fused_computation.59 | loop fusion | flops 1048576 | bytes 9437184 | tf_op jit(solution)/shard_map/concatenate | solution.py:106
  126.7 1.9 collective-permute-start.4
  128.6 18.3 %collective-permute-start.5 = (f32[256,1024]{0,1:T(8,128)}, f32[256,1024]{0,1:T(8,128)}, u32[]{:S(2)}, u32[]{:S(2)}) collective-permute-start(f32[256,1024]{0,1:T(8,128)} %get-tuple-element.127), channel_id=1, source_target_pairs={{4,0},{6,2},{8,4},{10,6},{12,8},{14,10},{16,12},{18,14},{20,16},{2... | collective-permute-start | bytes 3145736 | tf_op jit(solution)/shard_map/ppermute | solution.py:15
  146.9 1.9 collective-permute-start.7
  148.8 3.2 %collective-permute-start.6 = (f32[256,1024]{0,1:T(8,128)}, f32[256,1024]{0,1:T(8,128)}, u32[]{:S(2)}, u32[]{:S(2)}) collective-permute-start(f32[256,1024]{0,1:T(8,128)} %get-tuple-element.129), channel_id=1, source_target_pairs={{6,0},{8,2},{10,4},{12,6},{14,8},{16,10},{18,12},{20,14},{22,16},{... | collective-permute-start | bytes 3145736 | tf_op jit(solution)/shard_map/ppermute | solution.py:15
  152.7 1.2 convert_element_type.23
  153.8 6.9 %all_to_all.124 = bf16[2,128,1024]{2,1,0:T(8,128)(2,1)S(1)} all-to-all(bf16[2,128,1024]{2,1,0:T(8,128)(2,1)} %convert_element_type.23), channel_id=1, replica_groups=mesh['groups'=1,'blk'=16,'heads'=2] {'heads'}, dimensions={0} | all-to-all | bytes 1048576 | tf_op jit(solution)/shard_map/all_to_all | solution.py:117
  160.7 1.0 copy.47
  161.7 2.0 copy.54
  163.8 26.4 %collective-permute-done.5 = f32[256,1024]{0,1:T(8,128)} collective-permute-done((f32[256,1024]{0,1:T(8,128)}, f32[256,1024]{0,1:T(8,128)}, u32[]{:S(2)}, u32[]{:S(2)}) %collective-permute-start.5) | collective-permute-done | bytes 1048608 | tf_op jit(solution)/shard_map/ppermute | solution.py:15
  190.2 24.5 %collective-permute-done.7 = f32[256,1024]{0,1:T(8,128)} collective-permute-done((f32[256,1024]{0,1:T(8,128)}, f32[256,1024]{0,1:T(8,128)}, u32[]{:S(2)}, u32[]{:S(2)}) %collective-permute-start.7) | collective-permute-done | bytes 1048608 | tf_op jit(solution)/shard_map/ppermute | solution.py:15
  214.7 36.6 %collective-permute-done.6 = f32[256,1024]{0,1:T(8,128)} collective-permute-done((f32[256,1024]{0,1:T(8,128)}, f32[256,1024]{0,1:T(8,128)}, u32[]{:S(2)}, u32[]{:S(2)}) %collective-permute-start.6) | collective-permute-done | bytes 1048608 | tf_op jit(solution)/shard_map/ppermute | solution.py:15
  251.3 2.6 fusion.53
  254.1 5.7 %all_to_all.125 = bf16[2,128,512]{2,1,0:T(8,128)(2,1)S(1)} all-to-all(bf16[2,128,512]{2,1,0:T(8,128)(2,1)S(1)} %bitcast.182), channel_id=1, replica_groups=mesh['groups'=1,'blk'=16,'heads'=2] {'heads'}, dimensions={0} | all-to-all | bytes 524288 | tf_op jit(solution)/shard_map/all_to_all | solution.py:119
  259.9 0.9 copy.56
  260.9 3.9 %all_to_all.126 = bf16[2,128,512]{2,1,0:T(8,128)(2,1)S(1)} all-to-all(bf16[2,128,512]{2,1,0:T(8,128)(2,1)S(1)} %bitcast.185), channel_id=1, replica_groups=mesh['groups'=1,'blk'=16,'heads'=2] {'heads'}, dimensions={0} | all-to-all | bytes 524288 | tf_op jit(solution)/shard_map/all_to_all | solution.py:118
  265.1 0.9 copy.55
  (91 shorter events, 14.1 us)
Async XLA Ops:
  0.6 24.9 %copy-start.3 = (bf16[128,2048]{1,0:T(8,128)(2,1)S(1)}, bf16[128,2048]{1,0:T(8,128)(2,1)}, u32[]{:S(2)}) copy-start(bf16[128,2048]{1,0:T(8,128)(2,1)} %param.8) | copy-start | bytes 1572868
  2.5 6.0 %all-to-all-start.1 = ((bf16[128,2,512]{0,2,1:T(8,128)(2,1)}), bf16[128,2,512]{0,2,1:T(8,128)(2,1)S(1)}, u32[]{:S(2)}, u32[]{:S(2)}) async-start(bf16[128,2,512]{0,2,1:T(8,128)(2,1)} %bitcast.2), calls=%async_computation.1 | async-start | bytes 524288 | tf_op jit(solution)/shard_map/all_to_all | solution.py:72
  6.6 24.5 %copy-start.8 = (s32[32]{0:T(128)S(1)}, s32[32]{0:T(128)}, u32[]{:S(2)}) copy-start(s32[32]{0:T(128)} %param.13) | copy-start | bytes 388
  6.6 24.6 %copy-start.9 = (s32[32]{0:T(128)S(1)}, s32[32]{0:T(128)}, u32[]{:S(2)}) copy-start(s32[32]{0:T(128)} %param.12) | copy-start | bytes 388
  6.6 24.8 %copy-start.4 = (bf16[128,2048]{1,0:T(8,128)(2,1)S(1)}, bf16[128,2048]{1,0:T(8,128)(2,1)}, u32[]{:S(2)}) copy-start(bf16[128,2048]{1,0:T(8,128)(2,1)} %param.11) | copy-start | bytes 1572868
  8.5 4.7 %all-to-all-start.2 = ((bf16[128,2,512]{0,2,1:T(8,128)(2,1)}), bf16[128,2,512]{0,2,1:T(8,128)(2,1)S(1)}, u32[]{:S(2)}, u32[]{:S(2)}) async-start(bf16[128,2,512]{0,2,1:T(8,128)(2,1)} %bitcast.5), calls=%async_computation.2 | async-start | bytes 524288 | tf_op jit(solution)/shard_map/all_to_all | solution.py:73
  14.2 45.6 %collective-permute-start.3 = (bf16[256,1024]{1,0:T(8,128)(2,1)}, bf16[256,1024]{1,0:T(8,128)(2,1)S(1)}, u32[]{:S(2)}, u32[]{:S(2)}) collective-permute-start(bf16[256,1024]{1,0:T(8,128)(2,1)} %pad_maximum_fusion.1), channel_id=1, source_target_pairs={{0,2},{2,4},{4,6},{6,8},{8,10},{10,12},{12,14},{14,16},{16,18},{18... | collective-permute-start | bytes 1572872 | tf_op jit(solution)/shard_map/ppermute | solution.py:15
  17.3 41.4 %collective-permute-start.2 = (bf16[256,1024]{1,0:T(8,128)(2,1)}, bf16[256,1024]{1,0:T(8,128)(2,1)}, u32[]{:S(2)}, u32[]{:S(2)}) collective-permute-start(bf16[256,1024]{1,0:T(8,128)(2,1)} %pad_maximum_fusion.1), channel_id=1, source_target_pairs={{0,4},{2,6},{4,8},{6,10},{8,12},{10,14},{12,16},{14,18},{16,20},{1... | collective-permute-start | bytes 1572872 | tf_op jit(solution)/shard_map/ppermute | solution.py:15
  20.5 37.2 %collective-permute-start.1 = (bf16[256,1024]{1,0:T(8,128)(2,1)}, bf16[256,1024]{1,0:T(8,128)(2,1)}, u32[]{:S(2)}, u32[]{:S(2)}) collective-permute-start(bf16[256,1024]{1,0:T(8,128)(2,1)} %pad_maximum_fusion.1), channel_id=1, source_target_pairs={{0,6},{2,8},{4,10},{6,12},{8,14},{10,16},{12,18},{14,20},{16,22},{... | collective-permute-start | bytes 1572872 | tf_op jit(solution)/shard_map/ppermute | solution.py:15
  23.6 22.8 %collective-permute-start = (bf16[256,1024]{1,0:T(8,128)(2,1)}, bf16[256,1024]{1,0:T(8,128)(2,1)}, u32[]{:S(2)}, u32[]{:S(2)}) collective-permute-start(bf16[256,1024]{1,0:T(8,128)(2,1)} %pad_maximum_fusion.1), channel_id=1, source_target_pairs={{0,8},{2,10},{4,12},{6,14},{8,16},{10,18},{12,20},{14,22},{16,24},... | collective-permute-start | bytes 1572872 | tf_op jit(solution)/shard_map/ppermute | solution.py:15
  26.4 6.1 %all-to-all-start = ((bf16[128,2,1024]{2,0,1:T(8,128)(2,1)}), bf16[128,2,1024]{2,0,1:T(8,128)(2,1)S(1)}, u32[]{:S(2)}, u32[]{:S(2)}) async-start(bf16[128,2,1024]{2,0,1:T(8,128)(2,1)} %bitcast.120), calls=%async_computation | async-start | bytes 1048576 | tf_op jit(solution)/shard_map/all_to_all | solution.py:70
  32.5 5.2 %all-to-all-start.3 = ((bf16[128,2,1024]{2,0,1:T(8,128)(2,1)}), bf16[128,2,1024]{2,0,1:T(8,128)(2,1)S(1)}, u32[]{:S(2)}, u32[]{:S(2)}) async-start(bf16[128,2,1024]{2,0,1:T(8,128)(2,1)} %bitcast.119), calls=%async_computation.3 | async-start | bytes 1048576 | tf_op jit(solution)/shard_map/all_to_all | solution.py:75
  62.2 4.3 %copy-start.1 = (bf16[4,2,256,128]{3,1,0,2:T(2,128)(2,1)}, bf16[4,2,256,128]{3,1,0,2:T(2,128)(2,1)S(1)}, u32[]{:S(2)}) copy-start(bf16[4,2,256,128]{3,1,0,2:T(2,128)(2,1)S(1)} %get-tuple-element.229) | copy-start | bytes 1572868 | tf_op jit(solution)/shard_map/while
  69.3 2.4 copy-start.5
  72.3 0.8 copy-start.6
  74.8 2.5 copy-start.2
  77.3 4.3 %copy-start.1 = (bf16[4,2,256,128]{3,1,0,2:T(2,128)(2,1)}, bf16[4,2,256,128]{3,1,0,2:T(2,128)(2,1)S(1)}, u32[]{:S(2)}) copy-start(bf16[4,2,256,128]{3,1,0,2:T(2,128)(2,1)S(1)} %get-tuple-element.229) | copy-start | bytes 1572868 | tf_op jit(solution)/shard_map/while
  84.3 2.4 copy-start.5
  87.3 0.8 copy-start.6
  89.8 2.5 copy-start.2
  92.3 4.3 %copy-start.1 = (bf16[4,2,256,128]{3,1,0,2:T(2,128)(2,1)}, bf16[4,2,256,128]{3,1,0,2:T(2,128)(2,1)S(1)}, u32[]{:S(2)}) copy-start(bf16[4,2,256,128]{3,1,0,2:T(2,128)(2,1)S(1)} %get-tuple-element.229) | copy-start | bytes 1572868 | tf_op jit(solution)/shard_map/while
  99.3 2.4 copy-start.5
  102.3 0.8 copy-start.6
  104.8 2.5 copy-start.2
  107.3 4.3 %copy-start.1 = (bf16[4,2,256,128]{3,1,0,2:T(2,128)(2,1)}, bf16[4,2,256,128]{3,1,0,2:T(2,128)(2,1)S(1)}, u32[]{:S(2)}) copy-start(bf16[4,2,256,128]{3,1,0,2:T(2,128)(2,1)S(1)} %get-tuple-element.229) | copy-start | bytes 1572868 | tf_op jit(solution)/shard_map/while
  114.3 2.4 copy-start.5
  117.3 0.8 copy-start.6
  119.8 2.5 copy-start.2
  122.3 29.8 %copy-start.7 = (bf16[4,2,256,128]{3,2,1,0:T(8,128)(2,1)S(1)}, bf16[4,2,256,128]{3,2,1,0:T(8,128)(2,1)}, u32[]{:S(2)}) copy-start(bf16[4,2,256,128]{3,2,1,0:T(8,128)(2,1)} %get-tuple-element.52) | copy-start | bytes 1572868
  126.7 37.1 %collective-permute-start.4 = (f32[256,1024]{0,1:T(8,128)}, f32[256,1024]{0,1:T(8,128)}, u32[]{:S(2)}, u32[]{:S(2)}) collective-permute-start(f32[256,1024]{0,1:T(8,128)} %get-tuple-element.126), channel_id=1, source_target_pairs={{2,0},{4,2},{6,4},{8,6},{10,8},{12,10},{14,12},{16,14},{18,16},{20... | collective-permute-start | bytes 3145736 | tf_op jit(solution)/shard_map/ppermute | solution.py:15
  128.6 61.6 %collective-permute-start.5 = (f32[256,1024]{0,1:T(8,128)}, f32[256,1024]{0,1:T(8,128)}, u32[]{:S(2)}, u32[]{:S(2)}) collective-permute-start(f32[256,1024]{0,1:T(8,128)} %get-tuple-element.127), channel_id=1, source_target_pairs={{4,0},{6,2},{8,4},{10,6},{12,8},{14,10},{16,12},{18,14},{20,16},{2... | collective-permute-start | bytes 3145736 | tf_op jit(solution)/shard_map/ppermute | solution.py:15
  146.9 67.8 %collective-permute-start.7 = (f32[256,1024]{0,1:T(8,128)}, f32[256,1024]{0,1:T(8,128)}, u32[]{:S(2)}, u32[]{:S(2)}) collective-permute-start(f32[256,1024]{0,1:T(8,128)} %get-tuple-element.128), channel_id=1, source_target_pairs={{8,0},{10,2},{12,4},{14,6},{16,8},{18,10},{20,12},{22,14},{24,16},... | collective-permute-start | bytes 3145736 | tf_op jit(solution)/shard_map/ppermute | solution.py:15
  148.8 102.4 %collective-permute-start.6 = (f32[256,1024]{0,1:T(8,128)}, f32[256,1024]{0,1:T(8,128)}, u32[]{:S(2)}, u32[]{:S(2)}) collective-permute-start(f32[256,1024]{0,1:T(8,128)} %get-tuple-element.129), channel_id=1, source_target_pairs={{6,0},{8,2},{10,4},{12,6},{14,8},{16,10},{18,12},{20,14},{22,16},{... | collective-permute-start | bytes 3145736 | tf_op jit(solution)/shard_map/ppermute | solution.py:15
  152.1 99.2 %copy-start = (f32[4,1280,128]{1,2,0:T(8,128)S(1)}, f32[4,1280,128]{1,2,0:T(8,128)}, u32[]{:S(2)}) copy-start(f32[4,1280,128]{1,2,0:T(8,128)} %get-tuple-element.54) | copy-start | bytes 7864324
where the time goes:
time: 267 us; the launch traced here: 266 us
  waiting for transfers between devices  107 us (40%)
  starting transfers between devices  52.9 us (20%)
  matrix products  44.9 us (17%)
  local copies, waits for them, and re-layouts  33.6 us (13%)
  blocking collectives  16.5 us (6%)
  other arithmetic  9.48 us (4%)
    ppermute x8, waiting for transfers between devices, from_behind(): lax.ppermute(value, axis, [(source, source + steps) for source in range(l...  105 us
    ppermute x8, starting transfers between devices, from_behind(): lax.ppermute(value, axis, [(source, source + steps) for source in range(l...  36.7 us
    dot_general x4, matrix products, attend_group(): jnp.einsum('hqk,kd->hqd', probs_b, value_part, preferred_element_type=jnp...  10.9 us
    unnamed x21, local copies, waits for them, and re-layouts  10.7 us
    dot_general x4, matrix products, attend_group(): jnp.einsum('hqk,hqd->kd', probs_b, grad_part, preferred_element_type=jnp....  10 us
    sub x4, matrix products, attend_group(): expo = jnp.exp(scores - top)  9.85 us
    dot_general x4, matrix products, attend_group(): jnp.einsum('hqd,kd->hqk', grad_part, value_part, preferred_element_type=j...  9.66 us
    all_to_all x1, blocking collectives, per_device(): lax.all_to_all(query_grad, 'heads', split_axis=0, concat_axis=1, tiled=True)  6.87 us
  transfers between devices with their start and end apart: 12, of which 8 were waited for; matrix products, arithmetic and copies ran while one was open for 5% of the time, Pallas kernels for 0%

commit v1 on v0

v1 whole, which is shorter than its diff:
```python
import math

import jax
import jax.numpy as jnp
from jax import lax
from jax.experimental import pallas as pl
from jax.experimental.pallas import tpu as pltpu
from jax.sharding import PartitionSpec as P

HEAD = 128
SCALAR = 168
WINDOW = 1024
BLOCK = 128
WB = WINDOW // BLOCK
SCALE = SCALAR ** (-0.5)
LOG2E = math.log2(math.e)

NT = (((1,), (1,)), ((), ()))
NN = (((1,), (0,)), ((), ()))
TN = (((0,), (0,)), ((), ()))


def dot(a, b, dims):
    return lax.dot_general(a, b, dims, preferred_element_type=jnp.float32)


def pack_kernel(a_ref, b_ref, out_ref):
    heads = out_ref.shape[0]
    width = out_ref.shape[2] // 2
    for h in range(heads):
        out_ref[h, :, :width] = a_ref[:, h * width : (h + 1) * width]
        out_ref[h, :, width:] = b_ref[:, h * width : (h + 1) * width]


def pack(a, b, heads):
    tokens, cols = a.shape
    return pl.pallas_call(
        pack_kernel,
        out_shape=jax.ShapeDtypeStruct((heads, tokens, 2 * cols // heads), a.dtype),
    )(a, b)


def attend_kernel(
    chunk_ref, doc_ref, band_ref, qd_ref, own_ref, halo_ref,
    dq_ref, dkv_own_ref, dkv_halo_ref,
    keys, values, dk, dv,
):
    chunk = own_ref.shape[0] * BLOCK
    blocks = chunk // BLOCK
    q_heads = qd_ref.shape[2] // (2 * HEAD)
    for j in range(blocks):
        rows = slice(j * BLOCK, (j + 1) * BLOCK)
        late = slice(WINDOW + j * BLOCK, WINDOW + (j + 1) * BLOCK)
        keys[rows, :] = halo_ref[j, :, :HEAD]
        values[rows, :] = halo_ref[j, :, HEAD:]
        keys[late, :] = own_ref[j, :, :HEAD]
        values[late, :] = own_ref[j, :, HEAD:]
    dk[...] = jnp.zeros_like(dk)
    dv[...] = jnp.zeros_like(dv)
    first = chunk_ref[0] * blocks

    def one_block(i, carry):
        index = first + i
        own_band = band_ref[index]
        own_doc = doc_ref[index]
        reach = jnp.int32(0)
        for back in range(1, WB + 1):
            seen = (
                (back <= own_band)
                & (index >= back)
                & (doc_ref[jnp.maximum(index - back, 0)] == own_doc)
            )
            reach = reach + seen.astype(jnp.int32)

        def work(span_blocks):
            span = span_blocks * BLOCK
            start = pl.multiple_of((i + WB + 1 - span_blocks) * BLOCK, BLOCK)
            window = pl.ds(start, span)
            query = jnp.concatenate(
                [qd_ref[i, :, h * HEAD : (h + 1) * HEAD] for h in range(q_heads)], axis=0
            )
            grad = jnp.concatenate(
                [
                    qd_ref[i, :, (q_heads + h) * HEAD : (q_heads + h + 1) * HEAD]
                    for h in range(q_heads)
                ],
                axis=0,
            )
            rows = q_heads * BLOCK
            key = keys[window, :]
            value = values[window, :]
            scores = dot(key, query, NT)
            key_pos = lax.broadcasted_iota(jnp.int32, (span, rows), 0)
            query_pos = lax.broadcasted_iota(jnp.int32, (span, rows), 1) % BLOCK
            low = (span_blocks - 1 - reach) * BLOCK
            allowed = (key_pos >= low) & (key_pos <= query_pos + (span - BLOCK))
            scores = jnp.where(allowed, scores, -jnp.inf)
            top = jnp.max(scores, axis=0, keepdims=True)
            expo = jnp.exp2((scores - top) * (SCALE * LOG2E))
            probs = expo * (1.0 / jnp.sum(expo, axis=0, keepdims=True))
            probs_b = probs.astype(jnp.bfloat16)
            dprob = dot(value, grad, NT)
            delta = jnp.sum(probs_b.astype(jnp.float32) * dprob, axis=0, keepdims=True)
            dscore = (probs * (dprob - delta)).astype(jnp.bfloat16)
            dv[window, :] += dot(probs_b, grad, NN)
            dk[window, :] += dot(dscore, query, NN)
            query_grad = (dot(dscore, key, TN) * SCALE).astype(jnp.bfloat16)
            for h in range(q_heads):
                dq_ref[i, :, h * HEAD : (h + 1) * HEAD] = query_grad[
                    h * BLOCK : (h + 1) * BLOCK, :
                ]

        sizes = (3, 6, WB + 1)
        least = 0
        for size in sizes:
            pl.when((reach + 1 > least) & (reach + 1 <= size))(lambda size=size: work(size))
            least = size
        return carry

    lax.fori_loop(0, blocks, one_block, 0)
    for j in range(blocks):
        rows = slice(j * BLOCK, (j + 1) * BLOCK)
        late = slice(WINDOW + j * BLOCK, WINDOW + (j + 1) * BLOCK)
        dkv_halo_ref[j, :, :HEAD] = (dk[rows, :] * SCALE).astype(dkv_halo_ref.dtype)
        dkv_halo_ref[j, :, HEAD:] = dv[rows, :].astype(dkv_halo_ref.dtype)
        dkv_own_ref[j, :, :HEAD] = dk[late, :] * SCALE
        dkv_own_ref[j, :, HEAD:] = dv[late, :]


def attend(chunk_index, doc_ids, band, queries_grads, own, halo):
    blocks = own.shape[0]
    total = WINDOW + blocks * BLOCK
    smem = pl.BlockSpec(memory_space=pltpu.SMEM)
    vmem = pl.BlockSpec(memory_space=pltpu.VMEM)
    return pl.pallas_call(
        attend_kernel,
        in_specs=[smem] * 3 + [vmem] * 3,
        out_specs=[vmem] * 3,
        out_shape=[
            jax.ShapeDtypeStruct(
                (blocks, BLOCK, queries_grads.shape[2] // 2), jnp.bfloat16
            ),
            jax.ShapeDtypeStruct(own.shape, jnp.float32),
            jax.ShapeDtypeStruct(own.shape, jnp.bfloat16),
        ],
        scratch_shapes=[
            pltpu.VMEM((total, HEAD), jnp.bfloat16),
            pltpu.VMEM((total, HEAD), jnp.bfloat16),
            pltpu.VMEM((total, HEAD), jnp.float32),
            pltpu.VMEM((total, HEAD), jnp.float32),
        ],
        compiler_params=pltpu.CompilerParams(vmem_limit_bytes=40 * 1024 * 1024),
    )(chunk_index, doc_ids, band, queries_grads, own, halo)


def per_device(queries, keys, values, upstream, doc_ids, band):
    tokens = queries.shape[0]
    parts = WINDOW // tokens
    cores = lax.axis_size("heads")
    spans = lax.axis_size("blk")
    step = parts // cores
    axes = ("blk", "heads")
    groups = [
        [first * parts + member for member in range(parts)] for first in range(spans // step)
    ]

    def exchange(value):
        return lax.all_to_all(
            value, axes, split_axis=0, concat_axis=0, axis_index_groups=groups, tiled=True
        )

    kv = exchange(pack(keys, values, parts))
    halo = lax.ppermute(kv, "blk", [(s, s + step) for s in range(spans - step)])
    qd = exchange(pack(queries, upstream, parts))
    chunk_index = (lax.axis_index("blk") // step).astype(jnp.int32).reshape(1)
    dq, dkv_own, dkv_halo = attend(chunk_index, doc_ids, band, qd, kv, halo)
    spill = lax.ppermute(dkv_halo, "blk", [(s + step, s) for s in range(spans - step)])
    query_out = exchange(dq)
    dkv = exchange((dkv_own + spill.astype(jnp.float32)).astype(jnp.bfloat16))

    def merge(value):
        return value.transpose(1, 0, 2).reshape(tokens, -1)

    return merge(query_out), merge(dkv[:, :, :HEAD]), merge(dkv[:, :, HEAD:])


def solution(mesh):
    sharded = P(("groups", "blk", "heads"), None)
    return jax.shard_map(
        per_device,
        mesh=mesh,
        in_specs=(sharded,) * 4 + (P("groups"),) * 2,
        out_specs=(sharded,) * 3,
        check_vma=False,
    )
```

time: 267 us -> 80.9 us (0.30)
  the two profiles are of different devices: /device:TPU:19 before, /device:TPU:0 now
where the time goes in v1:
time: 80.9 us; the launch traced here: 80.5 us
  waiting for transfers between devices  40.3 us (50%)
  starting transfers between devices  20.9 us (26%)
  Pallas kernels  14.1 us (17%)
  local copies, waits for them, and re-layouts  3.49 us (4%)
  other arithmetic  0.92 us (1%)
    all_to_all x4, waiting for transfers between devices, exchange(): lax.all_to_all(value, axes, split_axis=0, concat_axis=0, axis_index_group...  27.7 us
    all_to_all x4, starting transfers between devices, exchange(): lax.all_to_all(value, axes, split_axis=0, concat_axis=0, axis_index_group...  16.1 us
    ppermute x1, waiting for transfers between devices, per_device(): lax.ppermute(dkv_halo, 'blk', [(s + step, s) for s in range(spans - step)])  12.6 us
    pallas_call x1, Pallas kernels, attend(): pl.pallas_call(attend_kernel, in_specs=[smem] * 3 + [vmem] * 3, out_specs...  9.92 us
    pallas_call x2, Pallas kernels, pack(): pl.pallas_call(pack_kernel, out_shape=jax.ShapeDtypeStruct((heads, tokens...  4.17 us
    ppermute x1, starting transfers between devices, per_device(): halo = lax.ppermute(kv, 'blk', [(s, s + step) for s in range(spans - step)])  3.54 us
    unnamed x7, local copies, waits for them, and re-layouts  2.73 us
  transfers between devices with their start and end apart: 6, of which 4 were waited for; matrix products, arithmetic and copies ran while one was open for 3% of the time, Pallas kernels for 3%

profile of v1, /device:TPU:0, one launch (start us, length us, event | category | flops | bytes accessed | tf_op | source)
XLA Modules:
  0.0 80.5 jit_solution(13169061018547901928)
XLA Ops:
  0.6 1.9 %shard_map.86 = bf16[8,128,256]{2,1,0:T(8,128)(2,1)} custom-call(bf16[128,1024]{1,0:T(8,128)(2,1)} %a_ref.3, bf16[128,1024]{1,0:T(8,128)(2,1)} %b_ref.3), custom_call_target="tpu_custom_call" | custom-call | tf_op jit(solution)/shard_map/pallas_call | solution.py:37
  2.5 5.2 %all-to-all-start.1 = ((bf16[8,128,256]{2,1,0:T(8,128)(2,1)}), bf16[8,128,256]{2,1,0:T(8,128)(2,1)S(1)}, u32[]{:S(2)}, u32[]{:S(2)}) async-start(bf16[8,128,256]{2,1,0:T(8,128)(2,1)} %shard_map.86), calls=%async_computation.1 | async-start | bytes 1048576 | tf_op jit(solution)/shard_map/all_to_all | solution.py:168
  7.7 2.3 %shard_map.85 = bf16[8,128,512]{2,1,0:T(8,128)(2,1)} custom-call(bf16[128,2048]{1,0:T(8,128)(2,1)} %a_ref.2, bf16[128,2048]{1,0:T(8,128)(2,1)} %b_ref.2), custom_call_target="tpu_custom_call" | custom-call | tf_op jit(solution)/shard_map/pallas_call | solution.py:37
  10.0 7.5 %all-to-all-done.1.own_ref = bf16[8,128,256]{2,1,0:T(8,128)(2,1)S(1)} async-done(((bf16[8,128,256]{2,1,0:T(8,128)(2,1)}), bf16[8,128,256]{2,1,0:T(8,128)(2,1)S(1)}, u32[]{:S(2)}, u32[]{:S(2)}) %all-to-all-start.1) | async-done | bytes 524320 | tf_op jit(solution)/shard_map/all_to_all | solution.py:168
  17.5 3.6 %all-to-all-start = ((bf16[8,128,512]{2,1,0:T(8,128)(2,1)}), bf16[8,128,512]{2,1,0:T(8,128)(2,1)S(1)}, u32[]{:S(2)}, u32[]{:S(2)}) async-start(bf16[8,128,512]{2,1,0:T(8,128)(2,1)} %shard_map.85), calls=%async_computation | async-start | bytes 2097152 | tf_op jit(solution)/shard_map/all_to_all | solution.py:168
  21.0 3.5 %collective-permute-start = (bf16[8,128,256]{2,1,0:T(8,128)(2,1)S(1)}, bf16[8,128,256]{2,1,0:T(8,128)(2,1)S(1)}, u32[]{:S(2)}, u32[]{:S(2)}) collective-permute-start(bf16[8,128,256]{2,1,0:T(8,128)(2,1)S(1)} %all-to-all-done.1.own_ref), channel_id=1, source_target_pairs={{0,8},{2,10},{4,12},{6,14},{8,16},{10,18},{12,20},{14,22},{16,24},... | collective-permute-start | bytes 1572872 | tf_op jit(solution)/shard_map/ppermute | solution.py:173
  24.6 0.0 copy-start
  24.6 0.0 copy-start.1
  24.6 11.7 %all-to-all-done.qd_ref = bf16[8,128,512]{2,1,0:T(8,128)(2,1)S(1)} async-done(((bf16[8,128,512]{2,1,0:T(8,128)(2,1)}), bf16[8,128,512]{2,1,0:T(8,128)(2,1)S(1)}, u32[]{:S(2)}, u32[]{:S(2)}) %all-to-all-start) | async-done | bytes 1048608 | tf_op jit(solution)/shard_map/all_to_all | solution.py:168
  36.4 0.0 collective-permute-done.halo_ref
  36.4 0.0 copy-done
  36.4 0.0 copy-done.1
  36.4 9.9 %shard_map.87 = (bf16[8,128,256]{2,1,0:T(8,128)(2,1)}, f32[8,128,256]{2,1,0:T(8,128)S(1)}, bf16[8,128,256]{2,1,0:T(8,128)(2,1)}) custom-call(s32[1]{0:T(128)} %bitcast.chunk_ref, s32[32]{0:T(128)S(1)} %copy-done, s32[32]{0:T(128)S(1)} %copy-done.1, bf16[8,128,512]{2,1,0:T(8,128)(2,1)S(1)} %all-to-all-done.qd_ref, ...), custom_call_target="tpu_custom_call" | custom-call | tf_op jit(solution)/shard_map/pallas_call | solution.py:135
  46.3 1.3 %collective-permute-start.1 = (bf16[8,128,256]{2,1,0:T(8,128)(2,1)}, bf16[8,128,256]{2,1,0:T(8,128)(2,1)S(1)}, u32[]{:S(2)}, u32[]{:S(2)}) collective-permute-start(bf16[8,128,256]{2,1,0:T(8,128)(2,1)} %get-tuple-element.8), channel_id=1, source_target_pairs={{8,0},{10,2},{12,4},{14,6},{16,8},{18,10},{20,12},{22,14},{24,16},... | collective-permute-start | bytes 1572872 | tf_op jit(solution)/shard_map/ppermute | solution.py:177
  47.6 3.7 %all-to-all-start.2 = ((bf16[8,128,256]{2,1,0:T(8,128)(2,1)}), bf16[8,128,256]{2,1,0:T(8,128)(2,1)S(1)}, u32[]{:S(2)}, u32[]{:S(2)}) async-start(bf16[8,128,256]{2,1,0:T(8,128)(2,1)} %get-tuple-element.6), calls=%async_computation.2 | async-start | bytes 1048576 | tf_op jit(solution)/shard_map/all_to_all | solution.py:168
  51.3 12.6 %collective-permute-done.1 = bf16[8,128,256]{2,1,0:T(8,128)(2,1)S(1)} collective-permute-done((bf16[8,128,256]{2,1,0:T(8,128)(2,1)}, bf16[8,128,256]{2,1,0:T(8,128)(2,1)S(1)}, u32[]{:S(2)}, u32[]{:S(2)}) %collective-permute-start.1) | collective-permute-done | bytes 524320 | tf_op jit(solution)/shard_map/ppermute | solution.py:177
  64.0 0.9 %add_convert_fusion = bf16[8,128,256]{2,1,0:T(8,128)(2,1)} fusion(f32[8,128,256]{2,1,0:T(8,128)S(1)} %get-tuple-element.7, bf16[8,128,256]{2,1,0:T(8,128)(2,1)S(1)} %collective-permute-done.1), kind=kLoop, calls=%fused_computation | loop fusion | flops 786432 | bytes 2097152 | tf_op jit(solution)/shard_map/convert_element_type | solution.py:179
  64.9 0.0 all-to-all-done.2
  64.9 3.6 %all-to-all-start.3 = ((bf16[8,128,256]{2,1,0:T(8,128)(2,1)}), bf16[8,128,256]{2,1,0:T(8,128)(2,1)S(1)}, u32[]{:S(2)}, u32[]{:S(2)}) async-start(bf16[8,128,256]{2,1,0:T(8,128)(2,1)} %add_convert_fusion), calls=%async_computation.3 | async-start | bytes 1048576 | tf_op jit(solution)/shard_map/all_to_all | solution.py:168
  68.5 0.3 copy.9
  68.8 1.0 %copy.12 = bf16[128,2048]{1,0:T(8,128)(2,1)} copy(bf16[128,2048]{0,1:T(8,128)(2,1)S(1)} %bitcast.10) | data formatting | bytes 1048576
  69.8 8.5 %all-to-all-done.3 = bf16[8,128,256]{2,1,0:T(8,128)(2,1)S(1)} async-done(((bf16[8,128,256]{2,1,0:T(8,128)(2,1)}), bf16[8,128,256]{2,1,0:T(8,128)(2,1)S(1)}, u32[]{:S(2)}, u32[]{:S(2)}) %all-to-all-start.3) | async-done | bytes 524320 | tf_op jit(solution)/shard_map/all_to_all | solution.py:168
  78.3 0.1 slice_bitcast_fusion
  78.4 0.2 copy.11
  78.6 0.9 %copy.14 = bf16[128,1024]{1,0:T(8,128)(2,1)} copy(bf16[128,1024]{0,1:T(8,128)(2,1)S(1)} %bitcast.11) | data formatting | bytes 524288
  79.5 0.2 copy.10
  79.6 0.9 %copy.13 = bf16[128,1024]{1,0:T(8,128)(2,1)} copy(bf16[128,1024]{0,1:T(8,128)(2,1)S(1)} %bitcast.12) | data formatting | bytes 524288
Async XLA Ops:
  2.5 14.9 %all-to-all-start.1 = ((bf16[8,128,256]{2,1,0:T(8,128)(2,1)}), bf16[8,128,256]{2,1,0:T(8,128)(2,1)S(1)}, u32[]{:S(2)}, u32[]{:S(2)}) async-start(bf16[8,128,256]{2,1,0:T(8,128)(2,1)} %shard_map.86), calls=%async_computation.1 | async-start | bytes 1048576 | tf_op jit(solution)/shard_map/all_to_all | solution.py:168
  17.5 18.9 %all-to-all-start = ((bf16[8,128,512]{2,1,0:T(8,128)(2,1)}), bf16[8,128,512]{2,1,0:T(8,128)(2,1)S(1)}, u32[]{:S(2)}, u32[]{:S(2)}) async-start(bf16[8,128,512]{2,1,0:T(8,128)(2,1)} %shard_map.85), calls=%async_computation | async-start | bytes 2097152 | tf_op jit(solution)/shard_map/all_to_all | solution.py:168
  21.0 15.3 %collective-permute-start = (bf16[8,128,256]{2,1,0:T(8,128)(2,1)S(1)}, bf16[8,128,256]{2,1,0:T(8,128)(2,1)S(1)}, u32[]{:S(2)}, u32[]{:S(2)}) collective-permute-start(bf16[8,128,256]{2,1,0:T(8,128)(2,1)S(1)} %all-to-all-done.1.own_ref), channel_id=1, source_target_pairs={{0,8},{2,10},{4,12},{6,14},{8,16},{10,18},{12,20},{14,22},{16,24},... | collective-permute-start | bytes 1572872 | tf_op jit(solution)/shard_map/ppermute | solution.py:173
  24.6 11.8 %copy-start = (s32[32]{0:T(128)S(1)}, s32[32]{0:T(128)}, u32[]{:S(2)}) copy-start(s32[32]{0:T(128)} %doc_ref.1) | copy-start | bytes 388
  24.6 11.8 %copy-start.1 = (s32[32]{0:T(128)S(1)}, s32[32]{0:T(128)}, u32[]{:S(2)}) copy-start(s32[32]{0:T(128)} %band_ref.1) | copy-start | bytes 388
  46.3 17.7 %collective-permute-start.1 = (bf16[8,128,256]{2,1,0:T(8,128)(2,1)}, bf16[8,128,256]{2,1,0:T(8,128)(2,1)S(1)}, u32[]{:S(2)}, u32[]{:S(2)}) collective-permute-start(bf16[8,128,256]{2,1,0:T(8,128)(2,1)} %get-tuple-element.8), channel_id=1, source_target_pairs={{8,0},{10,2},{12,4},{14,6},{16,8},{18,10},{20,12},{22,14},{24,16},... | collective-permute-start | bytes 1572872 | tf_op jit(solution)/shard_map/ppermute | solution.py:177
  47.6 17.3 %all-to-all-start.2 = ((bf16[8,128,256]{2,1,0:T(8,128)(2,1)}), bf16[8,128,256]{2,1,0:T(8,128)(2,1)S(1)}, u32[]{:S(2)}, u32[]{:S(2)}) async-start(bf16[8,128,256]{2,1,0:T(8,128)(2,1)} %get-tuple-element.6), calls=%async_computation.2 | async-start | bytes 1048576 | tf_op jit(solution)/shard_map/all_to_all | solution.py:168
  64.9 13.4 %all-to-all-start.3 = ((bf16[8,128,256]{2,1,0:T(8,128)(2,1)}), bf16[8,128,256]{2,1,0:T(8,128)(2,1)S(1)}, u32[]{:S(2)}, u32[]{:S(2)}) async-start(bf16[8,128,256]{2,1,0:T(8,128)(2,1)} %add_convert_fusion), calls=%async_computation.3 | async-start | bytes 1048576 | tf_op jit(solution)/shard_map/all_to_all | solution.py:168

commit v2 on v1

--- a/solution.py
+++ b/solution.py
@@ -1,3 +1,4 @@
+import functools
 import math
 
 import jax
@@ -34,10 +35,30 @@
 
 def pack(a, b, heads):
     tokens, cols = a.shape
+    vmem = pl.BlockSpec(memory_space=pltpu.VMEM)
     return pl.pallas_call(
         pack_kernel,
+        in_specs=[vmem] * 2,
+        out_specs=vmem,
         out_shape=jax.ShapeDtypeStruct((heads, tokens, 2 * cols // heads), a.dtype),
     )(a, b)
+
+
+def unpack_kernel(in_ref, *out_refs):
+    heads = in_ref.shape[0]
+    width = in_ref.shape[2] // len(out_refs)
+    for n, out_ref in enumerate(out_refs):
+        for h in range(heads):
+            out_ref[:, h * width : (h + 1) * width] = in_ref[h, :, n * width : (n + 1) * width]
+
+
+def unpack(value, outputs):
+    heads, tokens, width = value.shape
+    shape = jax.ShapeDtypeStruct((tokens, heads * width // outputs), value.dtype)
+    vmem = pl.BlockSpec(memory_space=pltpu.VMEM)
+    return pl.pallas_call(
+        unpack_kernel, in_specs=[vmem], out_specs=[vmem] * outputs, out_shape=[shape] * outputs
+    )(value)
 
 
 def attend_kernel(
@@ -89,19 +110,37 @@
             rows = q_heads * BLOCK
             key = keys[window, :]
             value = values[window, :]
-            scores = dot(key, query, NT)
-            key_pos = lax.broadcasted_iota(jnp.int32, (span, rows), 0)
-            query_pos = lax.broadcasted_iota(jnp.int32, (span, rows), 1) % BLOCK
-            low = (span_blocks - 1 - reach) * BLOCK
-            allowed = (key_pos >= low) & (key_pos <= query_pos + (span - BLOCK))
-            scores = jnp.where(allowed, scores, -jnp.inf)
-            top = jnp.max(scores, axis=0, keepdims=True)
-            expo = jnp.exp2((scores - top) * (SCALE * LOG2E))
-            probs = expo * (1.0 / jnp.sum(expo, axis=0, keepdims=True))
-            probs_b = probs.astype(jnp.bfloat16)
-            dprob = dot(value, grad, NT)
-            delta = jnp.sum(probs_b.astype(jnp.float32) * dprob, axis=0, keepdims=True)
-            dscore = (probs * (dprob - delta)).astype(jnp.bfloat16)
+
+            def split(x):
+                return [x[b * BLOCK : (b + 1) * BLOCK] for b in range(span_blocks)]
+
+            def fold(x):
+                return x.reshape(BLOCK // 8, 8, rows)
+
+            scores = split(dot(key, query, NT))
+            key_pos = lax.broadcasted_iota(jnp.int32, (BLOCK, rows), 0)
+            query_pos = lax.broadcasted_iota(jnp.int32, (BLOCK, rows), 1) % BLOCK
+            scores[-1] = jnp.where(key_pos <= query_pos, scores[-1], -jnp.inf)
+            top = functools.reduce(jnp.maximum, [jnp.max(fold(x), axis=0) for x in scores])
+            top = jnp.max(top, axis=0, keepdims=True)
+            dprob = split(dot(value, grad, NT))
+            expo = [jnp.exp2((x - top) * (SCALE * LOG2E)) for x in scores]
+            total = functools.reduce(jnp.add, [jnp.sum(fold(x), axis=0) for x in expo])
+            inverse = 1.0 / jnp.sum(total, axis=0, keepdims=True)
+            probs = [x * inverse for x in expo]
+            probs_b = [x.astype(jnp.bfloat16) for x in probs]
+            delta = functools.reduce(
+                jnp.add,
+                [
+                    jnp.sum(fold(x.astype(jnp.float32) * y), axis=0)
+                    for x, y in zip(probs_b, dprob)
+                ],
+            )
+            delta = jnp.sum(delta, axis=0, keepdims=True)
+            dscore = jnp.concatenate(
+                [(x * (y - delta)).astype(jnp.bfloat16) for x, y in zip(probs, dprob)], axis=0
+            )
+            probs_b = jnp.concatenate(probs_b, axis=0)
             dv[window, :] += dot(probs_b, grad, NN)
             dk[window, :] += dot(dscore, query, NN)
             query_grad = (dot(dscore, key, TN) * SCALE).astype(jnp.bfloat16)
@@ -110,11 +149,8 @@
                     h * BLOCK : (h + 1) * BLOCK, :
                 ]
 
-        sizes = (3, 6, WB + 1)
-        least = 0
-        for size in sizes:
-            pl.when((reach + 1 > least) & (reach + 1 <= size))(lambda size=size: work(size))
-            least = size
+        for size in range(1, WB + 2):
+            pl.when(reach + 1 == size)(functools.partial(work, size))
         return carry
 
     lax.fori_loop(0, blocks, one_block, 0)
@@ -178,10 +214,7 @@
     query_out = exchange(dq)
     dkv = exchange((dkv_own + spill.astype(jnp.float32)).astype(jnp.bfloat16))
 
-    def merge(value):
-        return value.transpose(1, 0, 2).reshape(tokens, -1)
-
-    return merge(query_out), merge(dkv[:, :, :HEAD]), merge(dkv[:, :, HEAD:])
+    return (*unpack(query_out, 1), *unpack(dkv, 2))
 
 
 def solution(mesh):

time: 80.9 us -> 79.7 us (0.985)
  Pallas kernels: 14.1 us -> 17.1 us
  local copies, waits for them, and re-layouts: 3.49 us -> 1.6 us
  waiting for transfers between devices: 40.3 us -> 38.6 us
    pallas_call x2 -> x4, Pallas kernels: 4.17 us -> 8.03 us  [the longest x2 4.18 us: pack(): pl.pallas_call(pack_kernel, in_specs=[vmem] * 2, out_specs=vmem, out_shap...]
    ppermute x1, waiting for transfers between devices: 12.6 us -> 11.5 us  [per_device(): lax.ppermute(dkv_halo, 'blk', [(s + step, s) for s in range(spans - step)])]
    unnamed x7 -> x8, local copies, waits for them, and re-layouts: 2.73 us -> 1.6 us
    pallas_call x1, Pallas kernels: 9.92 us -> 9.04 us  [attend(): pl.pallas_call(attend_kernel, in_specs=[smem] * 3 + [vmem] * 3, out_specs...]
  transfers between devices with their start and end apart: 6 -> 6, of which waited for: 4 -> 4; matrix products, arithmetic and copies ran while one was open for 3% -> 1% of each run, Pallas kernels for 3% -> 5%
where the time goes in v2:
time: 79.7 us; the launch traced here: 79.8 us
  waiting for transfers between devices  38.6 us (48%)
  starting transfers between devices  20.9 us (26%)
  Pallas kernels  17.1 us (21%)
  local copies, waits for them, and re-layouts  1.6 us (2%)
  other arithmetic  0.91 us (1%)
    all_to_all x4, waiting for transfers between devices, exchange(): lax.all_to_all(value, axes, split_axis=0, concat_axis=0, axis_index_group...  27.1 us
    all_to_all x4, starting transfers between devices, exchange(): lax.all_to_all(value, axes, split_axis=0, concat_axis=0, axis_index_group...  16.1 us
    ppermute x1, waiting for transfers between devices, per_device(): lax.ppermute(dkv_halo, 'blk', [(s + step, s) for s in range(spans - step)])  11.5 us
    pallas_call x1, Pallas kernels, attend(): pl.pallas_call(attend_kernel, in_specs=[smem] * 3 + [vmem] * 3, out_specs...  9.04 us
    pallas_call x2, Pallas kernels, pack(): pl.pallas_call(pack_kernel, in_specs=[vmem] * 2, out_specs=vmem, out_shap...  4.18 us
    pallas_call x2, Pallas kernels, unpack(): pl.pallas_call(unpack_kernel, in_specs=[vmem], out_specs=[vmem] * outputs...  3.85 us
    ppermute x1, starting transfers between devices, per_device(): halo = lax.ppermute(kv, 'blk', [(s, s + step) for s in range(spans - step)])  3.54 us
    unnamed x8, local copies, waits for them, and re-layouts  1.6 us
  transfers between devices with their start and end apart: 6, of which 4 were waited for; matrix products, arithmetic and copies ran while one was open for 1% of the time, Pallas kernels for 5%

profile of v2, /device:TPU:0, one launch (start us, length us, event | category | flops | bytes accessed | tf_op | source)
XLA Modules:
  0.0 79.8 jit_solution(4275060380318353367)
XLA Ops:
  0.6 1.9 %shard_map.86 = bf16[8,128,256]{2,1,0:T(8,128)(2,1)} custom-call(bf16[128,1024]{1,0:T(8,128)(2,1)} %a_ref.3, bf16[128,1024]{1,0:T(8,128)(2,1)} %b_ref.3), custom_call_target="tpu_custom_call" | custom-call | tf_op jit(solution)/shard_map/pallas_call | solution.py:39
  2.5 5.2 %all-to-all-start.1 = ((bf16[8,128,256]{2,1,0:T(8,128)(2,1)}), bf16[8,128,256]{2,1,0:T(8,128)(2,1)S(1)}, u32[]{:S(2)}, u32[]{:S(2)}) async-start(bf16[8,128,256]{2,1,0:T(8,128)(2,1)} %shard_map.86), calls=%async_computation.1 | async-start | bytes 1048576 | tf_op jit(solution)/shard_map/all_to_all | solution.py:204
  7.7 2.3 %shard_map.85 = bf16[8,128,512]{2,1,0:T(8,128)(2,1)} custom-call(bf16[128,2048]{1,0:T(8,128)(2,1)} %a_ref.2, bf16[128,2048]{1,0:T(8,128)(2,1)} %b_ref.2), custom_call_target="tpu_custom_call" | custom-call | tf_op jit(solution)/shard_map/pallas_call | solution.py:39
  10.0 7.5 %all-to-all-done.1.own_ref = bf16[8,128,256]{2,1,0:T(8,128)(2,1)S(1)} async-done(((bf16[8,128,256]{2,1,0:T(8,128)(2,1)}), bf16[8,128,256]{2,1,0:T(8,128)(2,1)S(1)}, u32[]{:S(2)}, u32[]{:S(2)}) %all-to-all-start.1) | async-done | bytes 524320 | tf_op jit(solution)/shard_map/all_to_all | solution.py:204
  17.5 3.6 %all-to-all-start = ((bf16[8,128,512]{2,1,0:T(8,128)(2,1)}), bf16[8,128,512]{2,1,0:T(8,128)(2,1)S(1)}, u32[]{:S(2)}, u32[]{:S(2)}) async-start(bf16[8,128,512]{2,1,0:T(8,128)(2,1)} %shard_map.85), calls=%async_computation | async-start | bytes 2097152 | tf_op jit(solution)/shard_map/all_to_all | solution.py:204
  21.0 3.5 %collective-permute-start = (bf16[8,128,256]{2,1,0:T(8,128)(2,1)S(1)}, bf16[8,128,256]{2,1,0:T(8,128)(2,1)S(1)}, u32[]{:S(2)}, u32[]{:S(2)}) collective-permute-start(bf16[8,128,256]{2,1,0:T(8,128)(2,1)S(1)} %all-to-all-done.1.own_ref), channel_id=1, source_target_pairs={{0,8},{2,10},{4,12},{6,14},{8,16},{10,18},{12,20},{14,22},{16,24},... | collective-permute-start | bytes 1572872 | tf_op jit(solution)/shard_map/ppermute | solution.py:209
  24.6 0.0 copy-start
  24.6 0.0 copy-start.1
  24.6 11.7 %all-to-all-done.qd_ref = bf16[8,128,512]{2,1,0:T(8,128)(2,1)S(1)} async-done(((bf16[8,128,512]{2,1,0:T(8,128)(2,1)}), bf16[8,128,512]{2,1,0:T(8,128)(2,1)S(1)}, u32[]{:S(2)}, u32[]{:S(2)}) %all-to-all-start) | async-done | bytes 1048608 | tf_op jit(solution)/shard_map/all_to_all | solution.py:204
  36.4 0.0 collective-permute-done.halo_ref
  36.4 0.0 copy-done
  36.4 0.0 copy-done.1
  36.4 9.0 %shard_map.87 = (bf16[8,128,256]{2,1,0:T(8,128)(2,1)}, f32[8,128,256]{2,1,0:T(8,128)S(1)}, bf16[8,128,256]{2,1,0:T(8,128)(2,1)}) custom-call(s32[1]{0:T(128)} %bitcast.chunk_ref, s32[32]{0:T(128)S(1)} %copy-done, s32[32]{0:T(128)S(1)} %copy-done.1, bf16[8,128,512]{2,1,0:T(8,128)(2,1)S(1)} %all-to-all-done.qd_ref, ...), custom_call_target="tpu_custom_call" | custom-call | tf_op jit(solution)/shard_map/pallas_call | solution.py:171
  45.4 1.3 %collective-permute-start.1 = (bf16[8,128,256]{2,1,0:T(8,128)(2,1)}, bf16[8,128,256]{2,1,0:T(8,128)(2,1)S(1)}, u32[]{:S(2)}, u32[]{:S(2)}) collective-permute-start(bf16[8,128,256]{2,1,0:T(8,128)(2,1)} %get-tuple-element.10), channel_id=1, source_target_pairs={{8,0},{10,2},{12,4},{14,6},{16,8},{18,10},{20,12},{22,14},{24,16},... | collective-permute-start | bytes 1572872 | tf_op jit(solution)/shard_map/ppermute | solution.py:213
  46.7 3.7 %all-to-all-start.2 = ((bf16[8,128,256]{2,1,0:T(8,128)(2,1)}), bf16[8,128,256]{2,1,0:T(8,128)(2,1)S(1)}, u32[]{:S(2)}, u32[]{:S(2)}) async-start(bf16[8,128,256]{2,1,0:T(8,128)(2,1)} %get-tuple-element.8), calls=%async_computation.2 | async-start | bytes 1048576 | tf_op jit(solution)/shard_map/all_to_all | solution.py:204
  50.5 11.5 %collective-permute-done.1 = bf16[8,128,256]{2,1,0:T(8,128)(2,1)S(1)} collective-permute-done((bf16[8,128,256]{2,1,0:T(8,128)(2,1)}, bf16[8,128,256]{2,1,0:T(8,128)(2,1)S(1)}, u32[]{:S(2)}, u32[]{:S(2)}) %collective-permute-start.1) | collective-permute-done | bytes 524320 | tf_op jit(solution)/shard_map/ppermute | solution.py:213
  61.9 0.9 %add_convert_fusion = bf16[8,128,256]{2,1,0:T(8,128)(2,1)} fusion(f32[8,128,256]{2,1,0:T(8,128)S(1)} %get-tuple-element.9, bf16[8,128,256]{2,1,0:T(8,128)(2,1)S(1)} %collective-permute-done.1), kind=kLoop, calls=%fused_computation | loop fusion | flops 786432 | bytes 2097152 | tf_op jit(solution)/shard_map/convert_element_type | solution.py:215
  62.8 0.0 all-to-all-done.2.in_ref
  62.8 0.0 copy-start.2
  62.8 0.8 copy-done.2
  63.6 3.6 %all-to-all-start.3 = ((bf16[8,128,256]{2,1,0:T(8,128)(2,1)}), bf16[8,128,256]{2,1,0:T(8,128)(2,1)S(1)}, u32[]{:S(2)}, u32[]{:S(2)}) async-start(bf16[8,128,256]{2,1,0:T(8,128)(2,1)} %add_convert_fusion), calls=%async_computation.3 | async-start | bytes 1048576 | tf_op jit(solution)/shard_map/all_to_all | solution.py:204
  67.3 1.9 %shard_map.88 = bf16[128,2048]{1,0:T(8,128)(2,1)} custom-call(bf16[8,128,256]{2,1,0:T(8,128)(2,1)} %copy-done.2), custom_call_target="tpu_custom_call" | custom-call | tf_op jit(solution)/shard_map/pallas_call | solution.py:59
  69.2 7.9 %all-to-all-done.3.in_ref = bf16[8,128,256]{2,1,0:T(8,128)(2,1)S(1)} async-done(((bf16[8,128,256]{2,1,0:T(8,128)(2,1)}), bf16[8,128,256]{2,1,0:T(8,128)(2,1)S(1)}, u32[]{:S(2)}, u32[]{:S(2)}) %all-to-all-start.3) | async-done | bytes 524320 | tf_op jit(solution)/shard_map/all_to_all | solution.py:204
  77.0 0.0 copy-start.3
  77.0 0.8 copy-done.3
  77.8 2.0 %shard_map.89 = (bf16[128,1024]{1,0:T(8,128)(2,1)}, bf16[128,1024]{1,0:T(8,128)(2,1)}) custom-call(bf16[8,128,256]{2,1,0:T(8,128)(2,1)} %copy-done.3), custom_call_target="tpu_custom_call" | custom-call | tf_op jit(solution)/shard_map/pallas_call | solution.py:59
Async XLA Ops:
  2.5 14.9 %all-to-all-start.1 = ((bf16[8,128,256]{2,1,0:T(8,128)(2,1)}), bf16[8,128,256]{2,1,0:T(8,128)(2,1)S(1)}, u32[]{:S(2)}, u32[]{:S(2)}) async-start(bf16[8,128,256]{2,1,0:T(8,128)(2,1)} %shard_map.86), calls=%async_computation.1 | async-start | bytes 1048576 | tf_op jit(solution)/shard_map/all_to_all | solution.py:204
  17.5 18.9 %all-to-all-start = ((bf16[8,128,512]{2,1,0:T(8,128)(2,1)}), bf16[8,128,512]{2,1,0:T(8,128)(2,1)S(1)}, u32[]{:S(2)}, u32[]{:S(2)}) async-start(bf16[8,128,512]{2,1,0:T(8,128)(2,1)} %shard_map.85), calls=%async_computation | async-start | bytes 2097152 | tf_op jit(solution)/shard_map/all_to_all | solution.py:204
  21.0 15.3 %collective-permute-start = (bf16[8,128,256]{2,1,0:T(8,128)(2,1)S(1)}, bf16[8,128,256]{2,1,0:T(8,128)(2,1)S(1)}, u32[]{:S(2)}, u32[]{:S(2)}) collective-permute-start(bf16[8,128,256]{2,1,0:T(8,128)(2,1)S(1)} %all-to-all-done.1.own_ref), channel_id=1, source_target_pairs={{0,8},{2,10},{4,12},{6,14},{8,16},{10,18},{12,20},{14,22},{16,24},... | collective-permute-start | bytes 1572872 | tf_op jit(solution)/shard_map/ppermute | solution.py:209
  24.6 11.8 %copy-start = (s32[32]{0:T(128)S(1)}, s32[32]{0:T(128)}, u32[]{:S(2)}) copy-start(s32[32]{0:T(128)} %doc_ref.1) | copy-start | bytes 388
  24.6 11.8 %copy-start.1 = (s32[32]{0:T(128)S(1)}, s32[32]{0:T(128)}, u32[]{:S(2)}) copy-start(s32[32]{0:T(128)} %band_ref.1) | copy-start | bytes 388
  45.4 16.5 %collective-permute-start.1 = (bf16[8,128,256]{2,1,0:T(8,128)(2,1)}, bf16[8,128,256]{2,1,0:T(8,128)(2,1)S(1)}, u32[]{:S(2)}, u32[]{:S(2)}) collective-permute-start(bf16[8,128,256]{2,1,0:T(8,128)(2,1)} %get-tuple-element.10), channel_id=1, source_target_pairs={{8,0},{10,2},{12,4},{14,6},{16,8},{18,10},{20,12},{22,14},{24,16},... | collective-permute-start | bytes 1572872 | tf_op jit(solution)/shard_map/ppermute | solution.py:213
  46.7 16.1 %all-to-all-start.2 = ((bf16[8,128,256]{2,1,0:T(8,128)(2,1)}), bf16[8,128,256]{2,1,0:T(8,128)(2,1)S(1)}, u32[]{:S(2)}, u32[]{:S(2)}) async-start(bf16[8,128,256]{2,1,0:T(8,128)(2,1)} %get-tuple-element.8), calls=%async_computation.2 | async-start | bytes 1048576 | tf_op jit(solution)/shard_map/all_to_all | solution.py:204
  62.8 0.8 %copy-start.2 = (bf16[8,128,256]{2,1,0:T(8,128)(2,1)}, bf16[8,128,256]{2,1,0:T(8,128)(2,1)S(1)}, u32[]{:S(2)}) copy-start(bf16[8,128,256]{2,1,0:T(8,128)(2,1)S(1)} %all-to-all-done.2.in_ref) | copy-start | bytes 1572868
  63.6 13.4 %all-to-all-start.3 = ((bf16[8,128,256]{2,1,0:T(8,128)(2,1)}), bf16[8,128,256]{2,1,0:T(8,128)(2,1)S(1)}, u32[]{:S(2)}, u32[]{:S(2)}) async-start(bf16[8,128,256]{2,1,0:T(8,128)(2,1)} %add_convert_fusion), calls=%async_computation.3 | async-start | bytes 1048576 | tf_op jit(solution)/shard_map/all_to_all | solution.py:204
  77.0 0.8 copy-start.3
